TPU v7x, 128 devices: a whole 4x4x4 slice. The times are simulated.
128 devices in a mesh: prompt: 4 (over z_lo, core), seq: 32 (over y, x, z_hi).
Axes of the slice: x: 4, y: 4, z: 4 (z_hi: 2, z_lo: 2; z = z_hi * 2 + z_lo), core: 2. Of those that a mesh axis runs over, the one named last changes fastest.
Arguments:
- resp_q: bfloat16 [32768, 8192], P(('prompt', 'seq')), may hold values from -8 to 8
- resp_k: bfloat16 [32768, 1024], P(('prompt', 'seq')), may hold values from -6 to 6
- resp_v: bfloat16 [32768, 1024], P(('prompt', 'seq')), may hold values from -6 to 6
- prefix_k: bfloat16 [4096, 1024], P(('prompt', 'seq')), may hold values from -6 to 6
- prefix_v: bfloat16 [4096, 1024], P(('prompt', 'seq')), may hold values from -6 to 6
- destination: int32 [32768], replicated, may hold values from 0 to 32767, as said below
- resp_len: int32 [4, 16], P('prompt'), may hold values from 1 to 768, 8192 in all within a row
Outputs:
- attended: bfloat16 [32768, 8192], P(('prompt', 'seq'))
Inputs may be any that keep to these rules, and one draw needn't show every extreme that they name: `destination`: A permutation of the 32768 positions; device i of the mesh (prompt index times 32 plus seq index) holds rollout rows i * 256 onwards and owns positions i * 256 onwards. From one device to one device go either exactly 2 rows or none.
All inputs are finite; a program needn't handle non-finite values.
Results may differ from a plain program's by a relative error of at most 0.0059.
Values may be sent and summed in bfloat16 or wider, within the bound.
A program may use at most 256 MiB of HBM per device.

v0:
```python
import math

import jax
import jax.numpy as jnp
from jax import lax
from jax.sharding import PartitionSpec as P

H = 64
KVH = 8
HD = 128


def from_behind(value, axis, steps):
    count = lax.axis_size(axis)
    first, last = (max(0, -steps), min(count, count - steps))
    return lax.ppermute(value, axis, [(source, source + steps) for source in range(first, last)])


def online_update(state, queries, key_blk, value_blk, allowed, scaling):
    run_max, run_sum, run_acc = state
    scores = (
        jnp.einsum("rkgd,nkd->rkgn", queries, key_blk, preferred_element_type=jnp.float32) * scaling
    )
    if allowed is not None:
        scores = jnp.where(allowed[:, None, None, :], scores, -jnp.inf)
    new_max = jnp.maximum(run_max, jnp.max(scores, axis=-1))
    shrink = jnp.exp(run_max - new_max)
    weights = jnp.exp(scores - new_max[..., None])
    run_sum = run_sum * shrink + jnp.sum(weights, axis=-1)
    update = jnp.einsum(
        "rkgn,nkd->rkgd",
        weights.astype(jnp.bfloat16),
        value_blk,
        preferred_element_type=jnp.float32,
    )
    run_acc = run_acc * shrink[..., None] + update
    return (new_max, run_sum, run_acc)


def select_rows(chooser, data):
    return jnp.dot(chooser, data, preferred_element_type=jnp.float32).astype(data.dtype)


def per_device(resp_q, resp_k, resp_v, prefix_k, prefix_v, destination, resp_len):
    n_seq = lax.axis_size("seq")
    n_prompt = lax.axis_size("prompt")
    n_devices = n_seq * n_prompt
    n_rows = resp_q.shape[0]
    capacity = 2 * ((n_rows + 2 * n_devices - 1) // (2 * n_devices))
    n_slots = n_devices * capacity
    my_index = lax.axis_index("prompt") * n_seq + lax.axis_index("seq")
    my_dest = lax.dynamic_slice_in_dim(destination, my_index * n_rows, n_rows)
    target = my_dest // n_rows
    row_ids = jnp.arange(n_rows, dtype=jnp.int32)
    before = (target[:, None] == target[None, :]) & (row_ids[None, :] < row_ids[:, None])
    slot_of = jnp.sum(before.astype(jnp.int32), axis=1)
    slot_index = target * capacity + slot_of
    slot_ids = jnp.arange(n_slots, dtype=jnp.int32)
    packer = (slot_ids[:, None] == slot_index[None, :]).astype(jnp.bfloat16)
    send_q = select_rows(packer, resp_q).reshape(n_devices, capacity, resp_q.shape[1])
    send_k = select_rows(packer, resp_k).reshape(n_devices, capacity, resp_k.shape[1])
    send_v = select_rows(packer, resp_v).reshape(n_devices, capacity, resp_v.shape[1])
    got_q, got_k, got_v = (
        lax.all_to_all(send_q, ("prompt", "seq"), split_axis=0, concat_axis=0, tiled=True),
        lax.all_to_all(send_k, ("prompt", "seq"), split_axis=0, concat_axis=0, tiled=True),
        lax.all_to_all(send_v, ("prompt", "seq"), split_axis=0, concat_axis=0, tiled=True),
    )
    got_q = got_q.reshape(n_slots, got_q.shape[-1])
    got_k = got_k.reshape(n_slots, got_k.shape[-1])
    got_v = got_v.reshape(n_slots, got_v.shape[-1])
    all_dest = destination.reshape(n_devices, n_rows)
    arrives = all_dest // n_rows == my_index
    lower = (row_ids[:, None] <= row_ids[None, :]).astype(jnp.float32)
    counted = jnp.dot(arrives.astype(jnp.float32), lower, preferred_element_type=jnp.float32)
    rank_of = counted.astype(jnp.int32) - 1
    source = jnp.arange(n_devices, dtype=jnp.int32)[:, None] * capacity + rank_of
    placed = jnp.where(arrives, all_dest % n_rows, n_rows).reshape(-1)
    source_flat = source.reshape(-1)
    lookup = jnp.sum(
        jnp.where(placed[None, :] == row_ids[:, None], source_flat[None, :], 0), axis=1
    )
    unpacker = (lookup[:, None] == slot_ids[None, :]).astype(jnp.bfloat16)
    q_rows = select_rows(unpacker, got_q)
    k_rows = select_rows(unpacker, got_k)
    v_rows = select_rows(unpacker, got_v)
    lengths = resp_len[0]
    finish = jnp.cumsum(lengths)
    scaling = 1.0 / math.sqrt(HD)
    per_kv = H // KVH
    seq_index = lax.axis_index("seq")
    queries = q_rows.reshape(n_rows, KVH, per_kv, HD)
    initial = (
        jnp.full((n_rows, KVH, per_kv), -jnp.inf, jnp.float32),
        jnp.zeros((n_rows, KVH, per_kv), jnp.float32),
        jnp.zeros((n_rows, KVH, per_kv, HD), jnp.float32),
    )
    keys_piece = lax.all_gather(prefix_k, "seq", axis=0, tiled=True)
    values_piece = lax.all_gather(prefix_v, "seq", axis=0, tiled=True)
    count = keys_piece.shape[0]
    width = math.gcd(count, 512)
    blocks = count // width
    stacked = (
        keys_piece.reshape(blocks, width, KVH, HD),
        values_piece.reshape(blocks, width, KVH, HD),
    )

    def inner(state, item):
        return (online_update(state, queries, item[0], item[1], None, scaling), None)

    state, unused = lax.scan(inner, initial, stacked)
    pairs = jnp.stack([k_rows, v_rows])
    windows = []
    for offset in (3, 2, 1):
        windows.append(from_behind(pairs, "seq", offset))
    windows.append(pairs)
    near = jnp.concatenate(windows, axis=1)
    key_ids = (seq_index - 3) * n_rows + jnp.arange(4 * n_rows, dtype=jnp.int32)
    query_ids = seq_index * n_rows + row_ids
    own_starts = jnp.sum(
        jnp.where(finish[None, :] <= query_ids[:, None], lengths[None, :], 0), axis=1
    )
    allowed = (key_ids[None, :] >= own_starts[:, None]) & (key_ids[None, :] <= query_ids[:, None])
    near_keys = near[0].reshape(4 * n_rows, KVH, HD)
    near_values = near[1].reshape(4 * n_rows, KVH, HD)
    state = online_update(state, queries, near_keys, near_values, allowed, scaling)
    run_max, run_sum, run_acc = state
    result = (run_acc / run_sum[..., None]).astype(jnp.bfloat16)
    return result.reshape(n_rows, H * HD)


def solution(mesh):
    return jax.shard_map(
        per_device,
        mesh=mesh,
        in_specs=(
            P(("prompt", "seq"), None),
            P(("prompt", "seq"), None),
            P(("prompt", "seq"), None),
            P(("prompt", "seq"), None),
            P(("prompt", "seq"), None),
            P(),
            P("prompt", None),
        ),
        out_specs=P(("prompt", "seq"), None),
        check_vma=False,
    )
```

profile of v0, /device:TPU:8, one launch (start us, length us, event | category | flops | bytes accessed | tf_op | source)
XLA Modules:
  0.0 471.9 jit_solution(2979927767456448673)
XLA Ops:
  6.5 0.7 all-gather.3.cloned.1.call-update
  7.3 0.8 and_select_fusion
  8.0 0.2 convert_reduce_fusion
  8.2 0.8 multiply_add_fusion.1
  9.0 0.3 convolution_convert_fusion.3
  9.3 1.0 reshape.167
  10.3 10.4 %all-to-all-start.2 = ((bf16[128,2,1024]{2,1,0:T(2,128)(2,1)}), bf16[128,2,1024]{2,1,0:T(2,128)(2,1)S(1)}, u32[]{:S(2)}, u32[]{:S(2)}) async-start(bf16[128,2,1024]{2,1,0:T(2,128)(2,1)} %reshape.167), calls=%async_computation.2 | async-start | bytes 1048576 | tf_op jit(solution)/shard_map/all_to_all | solution.py:66
  20.8 0.0 all-gather.5.cloned.1.call-start
  20.8 0.7 all-gather.5.cloned.1.call-update
  21.5 0.9 reshape.158
  22.5 1.4 convolution_convert_fusion.5
  23.8 1.0 reshape.165
  24.8 8.9 %all-to-all-done.2 = bf16[128,2,1024]{2,1,0:T(2,128)(2,1)S(1)} async-done(((bf16[128,2,1024]{2,1,0:T(2,128)(2,1)}), bf16[128,2,1024]{2,1,0:T(2,128)(2,1)S(1)}, u32[]{:S(2)}, u32[]{:S(2)}) %all-to-all-start.2) | async-done | bytes 524320 | tf_op jit(solution)/shard_map/all_to_all | solution.py:66
  33.7 5.6 %all-to-all-start.1 = ((bf16[128,2,1024]{2,1,0:T(2,128)(2,1)}), bf16[128,2,1024]{2,1,0:T(2,128)(2,1)S(1)}, u32[]{:S(2)}, u32[]{:S(2)}) async-start(bf16[128,2,1024]{2,1,0:T(2,128)(2,1)} %reshape.165), calls=%async_computation.1 | async-start | bytes 1048576 | tf_op jit(solution)/shard_map/all_to_all | solution.py:65
  39.3 5.5 %convolution_convert_fusion.1 = bf16[256,8192]{1,0:T(8,128)(2,1)} fusion(bf16[256,8192]{1,0:T(8,128)(2,1)} %param.9, s32[256]{0:T(256)S(1)} %multiply_add_fusion.1), kind=kOutput, calls=%fused_computation.30 | convolution fusion | flops 1075904512 | bytes 8389632 | tf_op jit(solution)/shard_map/dot_general | solution.py:41
  44.8 7.7 %reshape.159 = bf16[128,2,8192]{2,1,0:T(2,128)(2,1)} reshape(bf16[256,8192]{1,0:T(8,128)(2,1)} %convolution_convert_fusion.1) | data formatting | bytes 8388608 | tf_op jit(solution)/shard_map/reshape | solution.py:60
  52.4 10.9 %all-to-all-start = ((bf16[128,2,8192]{2,1,0:T(2,128)(2,1)}), bf16[128,2,8192]{2,1,0:T(2,128)(2,1)}, u32[]{:S(2)}, u32[]{:S(2)}) async-start(bf16[128,2,8192]{2,1,0:T(2,128)(2,1)} %reshape.159), calls=%async_computation | async-start | bytes 8388608 | tf_op jit(solution)/shard_map/all_to_all | solution.py:64
  63.4 0.2 fusion.30
  63.6 0.1 copy.48
  63.7 0.1 fusion.33
  63.9 5.5 %select_reduce_fusion = s32[256]{0:T(256)S(1)} fusion(s32[32768]{0:T(1024)S(1)} %bitcast.107, s32[32768]{0:T(1024)S(1)} %fusion.33), kind=kLoop, calls=%fused_computation.25 | loop fusion | flops 25165568 | bytes 263168 | tf_op jit(solution)/shard_map/reduce_sum | solution.py:79
  69.3 0.2 reshape.168
  69.5 0.2 reshape.166
  69.7 0.3 fusion.27
  70.1 0.3 fusion.26
  70.4 0.1 pad_maximum_fusion
  70.6 5.3 %collective-permute-start.2 = (bf16[2,256,1024]{2,1,0:T(8,128)(2,1)S(1)}, bf16[2,256,1024]{2,1,0:T(8,128)(2,1)}, u32[]{:S(2)}, u32[]{:S(2)}) collective-permute-start(bf16[2,256,1024]{2,1,0:T(8,128)(2,1)S(1)} %pad_maximum_fusion), channel_id=1, source_target_pairs={{0,1},{1,2},{2,3},{3,4},{4,5},{5,6},{6,7},{7,8},{8,9},{9,10},{10,1... | collective-permute-start | bytes 3145736 | tf_op jit(solution)/shard_map/ppermute | solution.py:16
  75.9 3.4 collective-permute-start.1
  79.3 3.7 collective-permute-start
  83.0 0.1 copy.30
  83.1 0.1 reduce
  83.3 0.1 select_reduce_fusion.1
  83.4 1.0 compare_and_fusion
  84.3 78.2 %collective-permute-done.2 = bf16[2,256,1024]{2,1,0:T(8,128)(2,1)} collective-permute-done((bf16[2,256,1024]{2,1,0:T(8,128)(2,1)S(1)}, bf16[2,256,1024]{2,1,0:T(8,128)(2,1)}, u32[]{:S(2)}, u32[]{:S(2)}) %collective-permute-start.2) | collective-permute-done | bytes 1048608 | tf_op jit(solution)/shard_map/ppermute | solution.py:16
  162.6 0.0 collective-permute-done.1
  162.6 45.8 %collective-permute-done = bf16[2,256,1024]{2,1,0:T(8,128)(2,1)} collective-permute-done((bf16[2,256,1024]{2,1,0:T(8,128)(2,1)S(1)}, bf16[2,256,1024]{2,1,0:T(8,128)(2,1)}, u32[]{:S(2)}, u32[]{:S(2)}) %collective-permute-start) | collective-permute-done | bytes 1048608 | tf_op jit(solution)/shard_map/ppermute | solution.py:16
  208.4 2.1 maximum_maximum_fusion
  210.5 2.0 fusion.62
  212.5 3.9 copy.44
  216.4 1.9 copy.51
  218.4 3.5 copy.47
  221.9 28.7 %all-gather.5.cloned.1.call-done = bf16[1024,1024]{1,0:T(8,128)(2,1)} async-done(((bf16[32,1024]{1,0:T(8,128)(2,1)}), bf16[1024,1024]{1,0:T(8,128)(2,1)}) %all-gather.5.cloned.1.call-update) | async-done | bytes 2097168 | tf_op jit(solution)/shard_map/all_gather | solution.py:98
  250.6 3.6 copy.50
  254.2 7.2 %reshape.160 = bf16[256,8192]{1,0:T(8,128)(2,1)} reshape(bf16[128,2,8192]{2,1,0:T(2,128)(2,1)} %all-to-all-done) | data formatting | bytes 8388608 | tf_op jit(solution)/shard_map/reshape | solution.py:68
  261.3 3.5 fusion.23
  264.8 1.2 copy.49
  266.0 2.0 copy-done.2
  268.0 4.7 copy.28
  272.7 103.3 %while.15 = (s32[]{:T(128)}, f32[256,8,8]{0,2,1:T(8,128)S(1)}, f32[256,8,8]{0,2,1:T(8,128)S(1)}, f32[256,8,8,128]{0,3,2,1:T(8,128)}, bf16[2,512,8,128]{3,2,1,0:T...) while((s32[]{:T(128)}, f32[256,8,8]{0,2,1:T(8,128)S(1)}, ...), condition=%wide.region_5.6_spmd.clone, body=%wide.region_2.5_spmd.clone.sunk | while | flops 4368449536 | bytes 131072112 | solution.py:110
  272.9 2.6 constant_dynamic-slice_fusion.3
  275.6 1.6 copy.67
  277.2 15.3 %bitcast_reduce_fusion.2 = (f32[256,8,8]{0,2,1:T(8,128)S(1)}, f32[8,512,256,8]{2,1,3,0:T(8,128)}) fusion(bf16[256,8,8,128]{3,0,2,1:T(8,128)(2,1)} %get-tuple-element.196, bf16[1,512,8,128]{3,2,1,0:T(8,128)(2,1)S(1)} %get-tuple-element.167), kind=kOutput, calls=%fused_computation.1.clone.1 | convolution fusion | flops 2164244480 | bytes 38862848 | tf_op jit(solution)/shard_map/while/body/eval_jaxpr/rkgd,nkd->rkgn/dot_general | solution.py:22
  292.6 13.6 %fusion.79 = f32[256,8,8]{0,2,1:T(8,128)S(1)} fusion(f32[8,512,256,8]{2,1,3,0:T(8,128)} %get-tuple-element.169, f32[256,8,8]{0,2,1:T(8,128)S(1)} %select_maximum_fusion.2), kind=kLoop, calls=%fused_computation.4.clone.1 | loop fusion | flops 25149440 | bytes 33685504 | tf_op jit(solution)/shard_map/while/body/eval_jaxpr/reduce_sum | solution.py:29
  306.2 16.5 %bitcast_add_fusion.3 = f32[256,8,8,128]{0,3,2,1:T(8,128)} fusion(f32[256,8,8,128]{0,3,2,1:T(8,128)} %get-tuple-element.185, f32[256,8,8]{0,2,1:T(8,128)S(1)} %get-tuple-element.171, pred[]{:T(512)S(6)} %compare.12, f32[8,512,256,8]{2,1,3,0:T(8,128)} %get-tuple-element.169, f32[256,8,8]{0,2,1:T(8,128)S(1)} %select_maximum_fusion.2, ...), kind=kOutput, calls=%fused_computation.8.clone.1 | convolution fusion | flops 2178940928 | bytes 51511296 | tf_op jit(solution)/shard_map/while/body/eval_jaxpr/rkgn,nkd->rkgd/dot_general | solution.py:30
  322.8 2.6 constant_dynamic-slice_fusion.3
  325.4 1.6 copy.67
  327.0 15.3 %bitcast_reduce_fusion.2 = (f32[256,8,8]{0,2,1:T(8,128)S(1)}, f32[8,512,256,8]{2,1,3,0:T(8,128)}) fusion(bf16[256,8,8,128]{3,0,2,1:T(8,128)(2,1)} %get-tuple-element.196, bf16[1,512,8,128]{3,2,1,0:T(8,128)(2,1)S(1)} %get-tuple-element.167), kind=kOutput, calls=%fused_computation.1.clone.1 | convolution fusion | flops 2164244480 | bytes 38862848 | tf_op jit(solution)/shard_map/while/body/eval_jaxpr/rkgd,nkd->rkgn/dot_general | solution.py:22
  342.4 13.6 %fusion.79 = f32[256,8,8]{0,2,1:T(8,128)S(1)} fusion(f32[8,512,256,8]{2,1,3,0:T(8,128)} %get-tuple-element.169, f32[256,8,8]{0,2,1:T(8,128)S(1)} %select_maximum_fusion.2), kind=kLoop, calls=%fused_computation.4.clone.1 | loop fusion | flops 25149440 | bytes 33685504 | tf_op jit(solution)/shard_map/while/body/eval_jaxpr/reduce_sum | solution.py:29
  356.0 20.0 %bitcast_add_fusion.3 = f32[256,8,8,128]{0,3,2,1:T(8,128)} fusion(f32[256,8,8,128]{0,3,2,1:T(8,128)} %get-tuple-element.185, f32[256,8,8]{0,2,1:T(8,128)S(1)} %get-tuple-element.171, pred[]{:T(512)S(6)} %compare.12, f32[8,512,256,8]{2,1,3,0:T(8,128)} %get-tuple-element.169, f32[256,8,8]{0,2,1:T(8,128)S(1)} %select_maximum_fusion.2, ...), kind=kOutput, calls=%fused_computation.8.clone.1 | convolution fusion | flops 2178940928 | bytes 51511296 | tf_op jit(solution)/shard_map/while/body/eval_jaxpr/rkgn,nkd->rkgd/dot_general | solution.py:30
  376.1 31.0 %fusion.15 = (f32[256,8,8]{0,2,1:T(8,128)S(1)}, f32[8,1024,256,8]{2,1,3,0:T(8,128)}) fusion(pred[256,1024]{0,1:T(8,128)(4,1)S(1)} %copy-done.3, bf16[256,8,8,128]{3,2,1,0:T(8,128)(2,1)} %bitcast.99, bf16[1024,8,128,1]{2,1,0,3:T(8,128)(2,1)} %bitcast.102), kind=kOutput, calls=%fused_computation.24 | convolution fusion | flops 4345282560 | bytes 73728000 | tf_op jit(solution)/shard_map/rkgd,nkd->rkgn/dot_general | solution.py:22
  407.1 21.7 %fusion.13 = f32[256,8,8]{0,2,1:T(8,128)S(1)} fusion(f32[8,1024,256,8]{2,1,3,0:T(8,128)} %get-tuple-element.117, f32[256,8,8]{0,2,1:T(8,128)S(1)} %max.6, pred[256,1024]{0,1:T(8,128)(4,1)S(1)} %copy-done.3), kind=kLoop, calls=%fused_computation.22 | loop fusion | flops 67092480 | bytes 67502080 | tf_op jit(solution)/shard_map/reduce_sum | solution.py:29
  428.9 0.0 copy-start.1
  428.9 29.5 %fusion.20 = bf16[256,8,8,128]{0,3,2,1:T(8,128)(2,1)} fusion(f32[256,8,8,128]{0,3,2,1:T(8,128)} %get-tuple-element.44, f32[256,8,8]{0,2,1:T(8,128)S(1)} %get-tuple-element.108, f32[256,8,8]{0,2,1:T(8,128)S(1)} %get-tuple-element.109, bf16[1024,8,128,1]{0,2,3,1:T(8,128)(2,1)S(1)} %bitcast.105, f32[8,1024,256,8]{2,1,3,0:T(8,128)} %get-tuple-element.117, ...), kind=kOutput, calls=%fused_computation.33 | convolution fusion | flops 4370464768 | bytes 82247680 | tf_op jit(solution)/shard_map/rkgn,nkd->rkgd/dot_general | solution.py:30
  458.4 6.3 %copy.35 = bf16[256,8192]{1,0:T(8,128)(2,1)} copy(bf16[256,8192]{0,1:T(8,128)(2,1)} %bitcast.103) | data formatting | bytes 8388608 | tf_op jit(solution)/shard_map/reshape | solution.py:128
  (31 shorter events, 0.2 us)
Async XLA Ops:
  6.5 2.5 copy-start
  6.5 211.8 %all-gather.3.cloned.1.call-start = ((), (), s32[]{:S(2)}) async-start(), calls=%async_computation.3 | async-start | bytes 2162688 | tf_op jit(solution)/shard_map/all_gather | solution.py:97
  10.3 23.4 %all-to-all-start.2 = ((bf16[128,2,1024]{2,1,0:T(2,128)(2,1)}), bf16[128,2,1024]{2,1,0:T(2,128)(2,1)S(1)}, u32[]{:S(2)}, u32[]{:S(2)}) async-start(bf16[128,2,1024]{2,1,0:T(2,128)(2,1)} %reshape.167), calls=%async_computation.2 | async-start | bytes 1048576 | tf_op jit(solution)/shard_map/all_to_all | solution.py:66
  20.8 229.8 %all-gather.5.cloned.1.call-start = ((), (), s32[]{:S(2)}) async-start(), calls=%async_computation.4 | async-start | bytes 2162688 | tf_op jit(solution)/shard_map/all_gather | solution.py:98
  33.7 18.7 %all-to-all-start.1 = ((bf16[128,2,1024]{2,1,0:T(2,128)(2,1)}), bf16[128,2,1024]{2,1,0:T(2,128)(2,1)S(1)}, u32[]{:S(2)}, u32[]{:S(2)}) async-start(bf16[128,2,1024]{2,1,0:T(2,128)(2,1)} %reshape.165), calls=%async_computation.1 | async-start | bytes 1048576 | tf_op jit(solution)/shard_map/all_to_all | solution.py:65
  44.8 18.9 %copy-start.5 = (s32[32768]{0:T(1024)S(1)}, s32[32768]{0:T(1024)}, u32[]{:S(2)}) copy-start(s32[32768]{0:T(1024)} %param.14) | copy-start | bytes 393220
  52.4 30.6 %copy-start.6 = (s32[1,16]{1,0:T(1,128)S(1)}, s32[1,16]{1,0:T(1,128)}, u32[]{:S(2)}) copy-start(s32[1,16]{1,0:T(1,128)} %param.15) | copy-start | bytes 196
  52.4 201.7 %all-to-all-start = ((bf16[128,2,8192]{2,1,0:T(2,128)(2,1)}), bf16[128,2,8192]{2,1,0:T(2,128)(2,1)}, u32[]{:S(2)}, u32[]{:S(2)}) async-start(bf16[128,2,8192]{2,1,0:T(2,128)(2,1)} %reshape.159), calls=%async_computation | async-start | bytes 8388608 | tf_op jit(solution)/shard_map/all_to_all | solution.py:64
  70.6 92.0 %collective-permute-start.2 = (bf16[2,256,1024]{2,1,0:T(8,128)(2,1)S(1)}, bf16[2,256,1024]{2,1,0:T(8,128)(2,1)}, u32[]{:S(2)}, u32[]{:S(2)}) collective-permute-start(bf16[2,256,1024]{2,1,0:T(8,128)(2,1)S(1)} %pad_maximum_fusion), channel_id=1, source_target_pairs={{0,1},{1,2},{2,3},{3,4},{4,5},{5,6},{6,7},{7,8},{8,9},{9,10},{10,1... | collective-permute-start | bytes 3145736 | tf_op jit(solution)/shard_map/ppermute | solution.py:16
  75.9 86.7 %collective-permute-start.1 = (bf16[2,256,1024]{2,1,0:T(8,128)(2,1)S(1)}, bf16[2,256,1024]{2,1,0:T(8,128)(2,1)}, u32[]{:S(2)}, u32[]{:S(2)}) collective-permute-start(bf16[2,256,1024]{2,1,0:T(8,128)(2,1)S(1)} %pad_maximum_fusion), channel_id=1, source_target_pairs={{0,2},{1,3},{2,4},{3,5},{4,6},{5,7},{6,8},{7,9},{8,10},{9,11},{10,... | collective-permute-start | bytes 3145736 | tf_op jit(solution)/shard_map/ppermute | solution.py:16
  79.3 129.1 %collective-permute-start = (bf16[2,256,1024]{2,1,0:T(8,128)(2,1)S(1)}, bf16[2,256,1024]{2,1,0:T(8,128)(2,1)}, u32[]{:S(2)}, u32[]{:S(2)}) collective-permute-start(bf16[2,256,1024]{2,1,0:T(8,128)(2,1)S(1)} %pad_maximum_fusion), channel_id=1, source_target_pairs={{0,3},{1,4},{2,5},{3,6},{4,7},{5,8},{6,9},{7,10},{8,11},{9,12},{10... | collective-permute-start | bytes 3145736 | tf_op jit(solution)/shard_map/ppermute | solution.py:16
  266.0 2.0 copy-start.2
  272.7 103.3 %copy-start.3 = (pred[256,1024]{0,1:T(8,128)(4,1)S(1)}, pred[256,1024]{0,1:T(8,128)(4,1)}, u32[]{:S(2)}) copy-start(pred[256,1024]{0,1:T(8,128)(4,1)} %compare_and_fusion) | copy-start | bytes 786436
  407.1 21.8 %copy-start.4 = (bf16[1,1024,1024]{1,2,0:T(8,128)(2,1)S(1)}, bf16[1,1024,1024]{1,2,0:T(8,128)(2,1)}, u32[]{:S(2)}) copy-start(bf16[1,1024,1024]{1,2,0:T(8,128)(2,1)} %copy.44) | copy-start | bytes 6291460
  428.9 35.9 %copy-start.1 = (bf16[256,1024]{1,0:T(8,128)(2,1)S(1)}, bf16[256,1024]{1,0:T(8,128)(2,1)}, u32[]{:S(2)}) copy-start(bf16[256,1024]{1,0:T(8,128)(2,1)} %param.11) | copy-start | bytes 1572868
Sparse Core Ops, SparseCore 0:
  10.4 164.5 all-gather.2
  177.9 72.6 all-gather.4
where the time goes:
time: 479 us; the launch traced here: 472 us
  waiting for transfers between devices  163 us (34%)
  matrix products  139 us (29%)
  other arithmetic  59.9 us (13%)
  local copies, waits for them, and re-layouts  56.1 us (12%)
  starting transfers between devices  39.4 us (8%)
  between operations  14 us (3%)
    ppermute x3, waiting for transfers between devices, from_behind(): lax.ppermute(value, axis, [(source, source + steps) for source in range(f...  124 us
    dot_general x3, matrix products, online_update(): jnp.einsum('rkgn,nkd->rkgd', weights.astype(jnp.bfloat16), value_blk, pre...  66 us
    dot_general x3, matrix products, online_update(): jnp.einsum('rkgd,nkd->rkgn', queries, key_blk, preferred_element_type=jnp...  61.7 us
    reduce_sum x3, other arithmetic, online_update(): run_sum = run_sum * shrink + jnp.sum(weights, axis=-1)  48.9 us
    all_gather x1, waiting for transfers between devices, per_device(): values_piece = lax.all_gather(prefix_v, 'seq', axis=0, tiled=True)  28.7 us
    unnamed x20, local copies, waits for them, and re-layouts  17 us
    ppermute x3, starting transfers between devices, from_behind(): lax.ppermute(value, axis, [(source, source + steps) for source in range(f...  12.4 us
    dot_general x6, matrix products, select_rows(): jnp.dot(chooser, data, preferred_element_type=jnp.float32)  11.3 us
  transfers between devices with their start and end apart: 8, of which 4 were waited for; matrix products, arithmetic and copies ran while one was open for 10% of the time, Pallas kernels for 0%

commit v1 on v0

v1 whole, which is shorter than its diff:
```python
import functools
import math

import jax
import jax.numpy as jnp
from jax import lax
from jax.experimental import pallas as pl
from jax.experimental.pallas import tpu as pltpu
from jax.sharding import PartitionSpec as P

MESH = pl.DeviceIdType.MESH
N = 128
NS = 32
ROWS = 256
GROUPS = 8
PER = 8
HD = 128
NEAR = 1024
PRE = 1024
KEYS = PRE + NEAR
WIDE = 512
SCALE = math.log2(math.e) / math.sqrt(HD)
BF = jnp.bfloat16
F32 = jnp.float32


def device_of(index):
    return (index // NS, lax.rem(index, NS))


def remote(src, dst, send, recv, device):
    return pltpu.make_async_remote_copy(
        src_ref=src, dst_ref=dst, send_sem=send, recv_sem=recv, device_id=device, device_id_type=MESH
    )


def await_bytes(ref, sem):
    pltpu.make_async_copy(ref, ref, sem).wait()


def iota(shape, dim):
    return lax.broadcasted_iota(jnp.int32, shape, dim).astype(F32)


def kernel(
    q_ref, k_ref, v_ref, pk_ref, pv_ref, dest_ref, dest_t_ref, len_ref, out_ref,
    send_q, send_kv, got_q, got_kv, pre_k, pre_v, stage_q, stage_kv, near,
    lhs, keys2, vals2, mask, back, scores, heads_out,
    q_send, q_recv, kv_send, kv_recv, pre_send, pre_recv,
):
    mp = lax.axis_index("prompt")
    ms = lax.axis_index("seq")
    me = mp * NS + ms
    my, mx, mz = ms // 8, lax.rem(ms // 2, 4), lax.rem(ms, 2)

    barrier = pltpu.get_barrier_semaphore()

    def greet(i, carry):
        pl.semaphore_signal(
            barrier, inc=1, device_id=device_of(lax.rem(me + i, N)), device_id_type=MESH
        )
        return carry

    lax.fori_loop(1, N, greet, 0)

    dest_t = dest_t_ref[...].astype(F32)
    own_row = dest_ref[pl.ds(me, 1), :].astype(F32)
    me_f = me.astype(F32)
    own_col = jnp.sum(jnp.where(iota((ROWS, N), 1) == me_f, dest_t, 0.0), axis=1, keepdims=True)
    slot = jnp.sum((own_col < own_row).astype(F32), axis=0, keepdims=True)
    packer = (iota((ROWS, ROWS), 0) == slot).astype(BF)

    send_kv[pl.ds(0, 96), :] = jnp.zeros((96, HD), BF)
    for half, ref in enumerate((k_ref, v_ref)):
        packed = jnp.dot(packer, ref[...], preferred_element_type=F32)
        for g in range(GROUPS):
            stage_kv[pl.ds(half * GROUPS + g, ROWS, stride=16), :] = packed[:, g * HD:(g + 1) * HD]
    send_kv[pl.ds(96, 4096), :] = stage_kv[...].astype(BF)
    pre_k[my, mx, mz] = pk_ref[...]
    pre_v[my, mx, mz] = pv_ref[...]
    got_kv[pl.ds(pl.multiple_of(me * 128, 128), 128), :] = send_kv[
        pl.ds(pl.multiple_of(me * 32, 32), 128), :
    ]

    def pack(g, carry):
        packed = jnp.dot(
            packer, q_ref[:, pl.ds(pl.multiple_of(g * 1024, 1024), 1024)],
            preferred_element_type=F32,
        )
        for j in range(PER):
            stage_q[pl.ds(j, ROWS, stride=PER), :] = packed[:, j * HD:(j + 1) * HD]
        send_q[g] = stage_q[...].astype(BF)
        own = pl.ds(pl.multiple_of(me * 16, 16), 16)
        got_q[g, own, :] = send_q[g, own, :]
        return carry

    lax.fori_loop(0, GROUPS, pack, 0)

    pl.semaphore_wait(barrier, N - 1)

    def along_x(k):
        return (mp, my * 8 + lax.rem(mx + k, 4) * 2 + mz)

    def along_y(k):
        return (mp, lax.rem(my + k, 4) * 8 + mx * 2 + mz)

    across = (mp, ms + 1 - 2 * mz)
    for i, ref in enumerate((pre_k, pre_v)):
        own = ref.at[my, mx, mz]
        remote(own, own, pre_send.at[i], pre_recv.at[i], across).start()

    def spread_kv(i, carry):
        to = lax.rem(me + i, N)
        remote(
            send_kv.at[pl.ds(pl.multiple_of(to * 32, 32), 128)],
            got_kv.at[pl.ds(pl.multiple_of(me * 128, 128), 128)],
            kv_send, kv_recv, device_of(to),
        ).start()
        return carry

    lax.fori_loop(1, N, spread_kv, 0)

    for i, ref in enumerate((pre_k, pre_v)):
        await_bytes(ref.at[0, 0, 0], pre_recv.at[i])
    for k in (1, 3, 2):
        remote(pre_k.at[my, mx], pre_k.at[my, mx], pre_send.at[2], pre_recv.at[2], along_x(k)).start()
        remote(pre_v.at[my, mx], pre_v.at[my, mx], pre_send.at[3], pre_recv.at[3], along_y(k)).start()

    def spread_q(n, carry):
        g, i = n // (N - 1), lax.rem(n, N - 1) + 1
        to = lax.rem(me + i, N)
        remote(
            send_q.at[g, pl.ds(pl.multiple_of(to * 16, 16), 16)],
            got_q.at[g, pl.ds(pl.multiple_of(me * 16, 16), 16)],
            q_send.at[g], q_recv.at[g], device_of(to),
        ).start()
        return carry

    lax.fori_loop(0, 2 * (N - 1), spread_q, 0)
    await_bytes(pre_k.at[0, pl.ds(0, 3)], pre_recv.at[2])
    await_bytes(pre_v.at[pl.ds(0, 3), 0], pre_recv.at[3])
    for k in (1, 3, 2):
        remote(pre_k.at[my], pre_k.at[my], pre_send.at[4], pre_recv.at[4], along_y(k)).start()
        remote(pre_v.at[:, mx], pre_v.at[:, mx], pre_send.at[5], pre_recv.at[5], along_x(k)).start()
    lax.fori_loop(2 * (N - 1), GROUPS * (N - 1), spread_q, 0)

    dest = dest_ref[...].astype(F32)
    base = me_f * ROWS
    here = (dest >= base) & (dest < base + ROWS)
    pos_q = jnp.concatenate(
        [
            jnp.min(jnp.where(here, dest, 1e9), axis=1, keepdims=True),
            jnp.max(jnp.where(here, dest, -1.0), axis=1, keepdims=True),
        ],
        axis=0,
    )
    prompt_base = (mp * (NS * ROWS)).astype(F32)
    start = jnp.zeros((ROWS, 1), F32) + prompt_base
    finish = prompt_base
    for c in range(16):
        length = len_ref[0, c].astype(F32)
        finish = finish + length
        start = start + jnp.where(pos_q >= finish, length, 0.0)
    pos_rows = []
    for k in range(4):
        low = base + (k - 3) * ROWS
        inside = (dest_t >= low) & (dest_t < low + ROWS)
        first = jnp.min(jnp.where(inside, dest_t, 1e9), axis=0, keepdims=True)
        last = jnp.max(jnp.where(inside, dest_t, -1.0), axis=0, keepdims=True)
        pos_rows.append((first, last))
    for k in range(4):
        for r in range(2):
            pos_k = pos_rows[k][r]
            mask[:, (2 * k + r) * N:(2 * k + r + 1) * N] = jnp.where(
                (pos_k >= start) & (pos_k <= pos_q), 0.0, -1e30
            )
    for r in range(2):
        back[:, r * N:(r + 1) * N] = (iota((ROWS, N), 0) == pos_rows[3][r] - base).astype(BF)
    vals2[:, HD:] = jnp.ones((KEYS, HD), BF)

    await_bytes(got_kv.at[pl.ds(0, (N - 1) * 128)], kv_recv)

    def unpack_kv(p, carry):
        stage_kv[...] = got_kv[pl.ds(pl.multiple_of(p * 4096, 4096), 4096), :].astype(F32)
        for x in range(16):
            for kr in range(8):
                near[x, pl.ds(pl.multiple_of(kr * N + p * 32, 32), 32), :] = stage_kv[
                    pl.ds(kr * 16 + x, 32, stride=128), :
                ].astype(BF)
        return carry

    lax.fori_loop(0, 4, unpack_kv, 0)
    await_bytes(pre_k.at[pl.ds(0, 3)], pre_recv.at[4])
    await_bytes(pre_v.at[:, pl.ds(0, 3)], pre_recv.at[5])

    def attend(g, carry):
        columns = pl.ds(pl.multiple_of(g * HD, HD), HD)
        for y in range(4):
            prefix_keys = pre_k[y, :, :, :, columns].reshape(256, HD)
            rows = pl.ds(y * 256, 256)
            keys2[rows, :HD] = prefix_keys
            keys2[rows, HD:] = prefix_keys
            vals2[rows, :HD] = pre_v[y, :, :, :, columns].reshape(256, HD)
        keys2[PRE:, :HD] = near[g]
        keys2[PRE:, HD:] = near[g]
        vals2[PRE:, :HD] = near[GROUPS + g]
        await_bytes(got_q.at[g, pl.ds(0, (N - 1) * 16)], q_recv.at[g])
        stage_q[...] = got_q[g].astype(F32)
        for j in range(PER):
            for r in range(2):
                scaled = stage_q[pl.ds(r * PER + j, N, stride=16), :] * SCALE
                high = scaled.astype(BF)
                lhs[j, r * N:(r + 1) * N, :HD] = high
                lhs[j, r * N:(r + 1) * N, HD:] = (scaled - high.astype(F32)).astype(BF)

        def head(j, inner):
            queries = lhs[j]
            top = None
            for c in range(KEYS // WIDE):
                part = lax.dot_general(
                    queries, keys2[c * WIDE:(c + 1) * WIDE, :], (((1,), (1,)), ((), ())),
                    preferred_element_type=F32,
                )
                if c * WIDE >= PRE:
                    part = part + mask[:, c * WIDE - PRE:(c + 1) * WIDE - PRE]
                scores[:, c * WIDE:(c + 1) * WIDE] = part
                for t in range(WIDE // HD):
                    tile = part[:, t * HD:(t + 1) * HD]
                    top = tile if top is None else jnp.maximum(top, tile)
            top = jnp.max(top, axis=1, keepdims=True)
            total = jnp.zeros((ROWS, 2 * HD), F32)
            for c in range(KEYS // WIDE):
                weights = jnp.exp2(scores[:, c * WIDE:(c + 1) * WIDE] - top).astype(BF)
                total = total + jnp.dot(
                    weights, vals2[c * WIDE:(c + 1) * WIDE, :], preferred_element_type=F32
                )
            heads_out[:, pl.ds(pl.multiple_of(j * HD, HD), HD)] = (
                total[:, :HD] / total[:, HD:]
            ).astype(BF)
            return inner

        lax.fori_loop(0, PER, head, 0)
        out_ref[:, pl.ds(pl.multiple_of(g * 1024, 1024), 1024)] = jnp.dot(
            back[...], heads_out[...], preferred_element_type=F32
        ).astype(BF)
        return carry

    lax.fori_loop(0, GROUPS, attend, 0)

    def sent_q(g, carry):
        await_bytes(send_q.at[g, pl.ds(0, (N - 1) * 16)], q_send.at[g])
        return carry

    lax.fori_loop(0, GROUPS, sent_q, 0)
    await_bytes(got_kv.at[pl.ds(0, (N - 1) * 128)], kv_send)
    for i, ref in enumerate((pre_k, pre_v)):
        await_bytes(ref.at[0, 0, 0], pre_send.at[i])
    await_bytes(pre_k.at[0, pl.ds(0, 3)], pre_send.at[2])
    await_bytes(pre_v.at[pl.ds(0, 3), 0], pre_send.at[3])
    await_bytes(pre_k.at[pl.ds(0, 3)], pre_send.at[4])
    await_bytes(pre_v.at[:, pl.ds(0, 3)], pre_send.at[5])


def per_device(resp_q, resp_k, resp_v, prefix_k, prefix_v, destination, resp_len):
    dest = destination.reshape(N, ROWS)
    vmem = pl.BlockSpec(memory_space=pltpu.VMEM)
    return pl.pallas_call(
        kernel,
        out_shape=jax.ShapeDtypeStruct((ROWS, GROUPS * PER * HD), BF),
        in_specs=[vmem] * 7 + [pl.BlockSpec(memory_space=pltpu.SMEM)],
        out_specs=vmem,
        scratch_shapes=[
            pltpu.VMEM((GROUPS, N * 16, HD), BF),
            pltpu.VMEM((131 * 32, HD), BF),
            pltpu.VMEM((GROUPS, N * 16, HD), BF),
            pltpu.VMEM((N * 128, HD), BF),
            pltpu.VMEM((4, 4, 2, 32, 1024), BF),
            pltpu.VMEM((4, 4, 2, 32, 1024), BF),
            pltpu.VMEM((N * 16, HD), F32),
            pltpu.VMEM((N * 32, HD), F32),
            pltpu.VMEM((16, NEAR, HD), BF),
            pltpu.VMEM((PER, ROWS, 2 * HD), BF),
            pltpu.VMEM((KEYS, 2 * HD), BF),
            pltpu.VMEM((KEYS, 2 * HD), BF),
            pltpu.VMEM((ROWS, NEAR), F32),
            pltpu.VMEM((ROWS, ROWS), BF),
            pltpu.VMEM((ROWS, KEYS), F32),
            pltpu.VMEM((ROWS, PER * HD), BF),
            pltpu.SemaphoreType.DMA((GROUPS,)),
            pltpu.SemaphoreType.DMA((GROUPS,)),
            pltpu.SemaphoreType.DMA,
            pltpu.SemaphoreType.DMA,
            pltpu.SemaphoreType.DMA((6,)),
            pltpu.SemaphoreType.DMA((6,)),
        ],
        compiler_params=pltpu.CompilerParams(
            collective_id=0, has_side_effects=True, vmem_limit_bytes=60 * 1024 * 1024
        ),
    )(resp_q, resp_k, resp_v, prefix_k, prefix_v, dest, dest.T, resp_len)


def solution(mesh):
    both = P(("prompt", "seq"), None)
    return jax.shard_map(
        per_device,
        mesh=mesh,
        in_specs=(both, both, both, both, both, P(), P("prompt", None)),
        out_specs=both,
        check_vma=False,
    )
```

time: 479 us -> 245 us (0.51)
  the two profiles are of different devices: /device:TPU:8 before, /device:TPU:24 now
where the time goes in v1:
time: 245 us
  Pallas kernels  238 us (97%)
  local copies, waits for them, and re-layouts  6.34 us (3%)
    pallas_call x1, Pallas kernels, per_device(): pl.pallas_call(kernel, out_shape=jax.ShapeDtypeStruct((ROWS, GROUPS * PER...  238 us

profile of v1, /device:TPU:24, one launch (start us, length us, event | category | flops | bytes accessed | tf_op | source)
XLA Modules:
  0.0 244.8 jit_solution(9549611121782046208)
XLA Ops:
  0.0 0.9 reshape.3.dest_ref
  0.9 0.0 copy-start
  1.0 0.8 copy.9
  1.7 0.0 copy-done
  1.7 238.4 %shard_map.73 = bf16[256,8192]{1,0:T(8,128)(2,1)} custom-call(bf16[256,8192]{1,0:T(8,128)(2,1)} %q_ref.1, bf16[256,1024]{1,0:T(8,128)(2,1)} %k_ref.1, bf16[256,1024]{1,0:T(8,128)(2,1)} %v_ref.1, bf16[32,1024]{1,0:T(8,128)(2,1)} %pk_ref.1, bf16[32,1024]{1,0:T(8,128)(2,1)} %pv_ref.1, s32[128,256]{1,0:T(8,128)} %copy-done, s32[256,128]{1,0:T(8,128)} %bitcast.1, ...), custom_call_target="tpu_custom_call" | custom-call | tf_op jit(solution)/shard_map/pallas_call | solution.py:267
  240.1 4.6 %copy.11 = bf16[256,8192]{1,0:T(8,128)(2,1)} copy(bf16[256,8192]{1,0:T(8,128)(2,1)} %shard_map.73) | data formatting | bytes 8388608
Async XLA Ops:
  0.9 0.8 copy-start

commit v2 on v1

v2 whole, which is shorter than its diff:
```python
import functools
import math

import jax
import jax.numpy as jnp
from jax import lax
from jax.experimental import pallas as pl
from jax.experimental.pallas import tpu as pltpu
from jax.sharding import PartitionSpec as P

MESH = pl.DeviceIdType.MESH
N = 128
NS = 32
ROWS = 256
GROUPS = 8
PER = 8
HD = 128
NEAR = 1024
PRE = 1024
KEYS = PRE + NEAR
WIDE = 256
TILE = 512
TILES = PER * ROWS // TILE
SCALE = math.log2(math.e) / math.sqrt(HD)
HALF = 4
LATE = 8
BF = jnp.bfloat16
F32 = jnp.float32


def device_of(index):
    return (index >> 5, index & (NS - 1))


def remote(src, dst, send, recv, device):
    return pltpu.make_async_remote_copy(
        src_ref=src, dst_ref=dst, send_sem=send, recv_sem=recv, device_id=device, device_id_type=MESH
    )


def await_bytes(ref, sem):
    pltpu.make_async_copy(ref, ref, sem).wait()


def iota(shape, dim):
    return lax.broadcasted_iota(jnp.int32, shape, dim).astype(F32)


def kernel(
    q_ref, k_ref, v_ref, pk_ref, pv_ref, dest_ref, dest_t_ref, len_ref, out_ref,
    send_q, send_kv, got_q, got_kv, pre_k, pre_v, stage_q, stage_kv, near,
    lhs, keys2, vals2, mask, back, scores_a, scores_b, peak_a, peak_b, heads_out,
    q_send, q_recv, kv_send, kv_recv, pre_send, pre_recv,
):
    mp = lax.axis_index("prompt")
    ms = lax.axis_index("seq")
    me = mp * NS + ms
    my, mx, mz = ms // 8, lax.rem(ms // 2, 4), lax.rem(ms, 2)

    barrier = pltpu.get_barrier_semaphore()

    def greet(i, carry):
        pl.semaphore_signal(
            barrier, inc=1, device_id=device_of((me + i) & (N - 1)), device_id_type=MESH
        )
        return carry

    lax.fori_loop(1, N, greet, 0)

    dest_t = dest_t_ref[...].astype(F32)
    own_row = dest_ref[pl.ds(me, 1), :].astype(F32)
    me_f = me.astype(F32)
    own_col = jnp.sum(jnp.where(iota((ROWS, N), 1) == me_f, dest_t, 0.0), axis=1, keepdims=True)
    slot = jnp.sum((own_col < own_row).astype(F32), axis=0, keepdims=True)
    packer = (iota((ROWS, ROWS), 0) == slot).astype(BF)

    for i, ref in enumerate((k_ref, v_ref)):
        packed = jnp.dot(packer, ref[...], preferred_element_type=F32)
        for g in range(GROUPS):
            stage_kv[g // HALF, pl.ds(i * HALF + g % HALF, ROWS, stride=8), :] = packed[
                :, g * HD:(g + 1) * HD
            ]
    for h in range(2):
        send_kv[h, pl.ds(0, 48), :] = jnp.zeros((48, HD), BF)
        send_kv[h, pl.ds(48, 2048), :] = stage_kv[h].astype(BF)
        got_kv[h, pl.ds(pl.multiple_of(me * 64, 64), 64), :] = send_kv[
            h, pl.ds(pl.multiple_of(me * 16, 16), 64), :
        ]
        pre_k[h, my, mx, mz] = pk_ref[:, h * HALF * HD:(h + 1) * HALF * HD]
        pre_v[h, my, mx, mz] = pv_ref[:, h * HALF * HD:(h + 1) * HALF * HD]

    pl.semaphore_wait(barrier, N - 1)

    def along_x(k):
        return (mp, my * 8 + lax.rem(mx + k, 4) * 2 + mz)

    def along_y(k):
        return (mp, lax.rem(my + k, 4) * 8 + mx * 2 + mz)

    across = (mp, ms + 1 - 2 * mz)
    for i, ref in enumerate((pre_k, pre_v)):
        own = ref.at[:, my, mx, mz]
        remote(own, own, pre_send.at[i], pre_recv.at[i], across).start()

    def spread_kv(h, i):
        to = (me + i) & (N - 1)
        remote(
            send_kv.at[h, pl.ds(pl.multiple_of(to * 16, 16), 64)],
            got_kv.at[h, pl.ds(pl.multiple_of(me * 64, 64), 64)],
            kv_send.at[h], kv_recv.at[h], device_of(to),
        ).start()

    def spread_kv_part(h, first, last):
        def one(i, carry):
            spread_kv(h, i)
            return carry

        lax.fori_loop(first, last, one, 0, unroll=4)

    def spread_prefix(h, first):
        def one(n, carry):
            k, b = (n >> 2) + 1, n & 3
            piece = pre_k.at[h, my, b]
            remote(piece, piece, pre_send.at[4 + 2 * h], pre_recv.at[4 + 2 * h], along_y(k)).start()
            spread_kv(h, first + 2 * n)
            piece = pre_v.at[h, b, mx]
            remote(piece, piece, pre_send.at[5 + 2 * h], pre_recv.at[5 + 2 * h], along_x(k)).start()
            spread_kv(h, first + 2 * n + 1)
            return carry

        lax.fori_loop(0, 12, one, 0)

    spread_kv_part(0, 1, 41)
    for i, ref in enumerate((pre_k, pre_v)):
        await_bytes(ref.at[:, 0, 0, 0], pre_recv.at[i])
    for k in (1, 3, 2):
        piece = pre_k.at[:, my, mx]
        remote(piece, piece, pre_send.at[2], pre_recv.at[2], along_x(k)).start()
        piece = pre_v.at[:, my, mx]
        remote(piece, piece, pre_send.at[3], pre_recv.at[3], along_y(k)).start()
    spread_kv_part(0, 41, 81)

    def pack(g, carry):
        packed = jnp.dot(
            packer, q_ref[:, pl.ds(pl.multiple_of(g * 1024, 1024), 1024)],
            preferred_element_type=F32,
        )
        for j in range(PER):
            stage_q[pl.ds(j, ROWS, stride=PER), :] = packed[:, j * HD:(j + 1) * HD]
        send_q[g] = stage_q[...].astype(BF)
        own = pl.ds(pl.multiple_of(me * 16, 16), 16)
        got_q[g, own, :] = send_q[g, own, :]
        return carry

    lax.fori_loop(0, GROUPS, pack, 0)

    dest = dest_ref[...].astype(F32)
    base = me_f * ROWS
    here = (dest >= base) & (dest < base + ROWS)
    pos_q = jnp.concatenate(
        [
            jnp.min(jnp.where(here, dest, 1e9), axis=1, keepdims=True),
            jnp.max(jnp.where(here, dest, -1.0), axis=1, keepdims=True),
        ],
        axis=0,
    )
    prompt_base = (mp * (NS * ROWS)).astype(F32)
    start = jnp.zeros((ROWS, 1), F32) + prompt_base
    finish = prompt_base
    for c in range(16):
        length = len_ref[0, c].astype(F32)
        finish = finish + length
        start = start + jnp.where(pos_q >= finish, length, 0.0)
    pos_rows = []
    for k in range(4):
        low = base + (k - 3) * ROWS
        inside = (dest_t >= low) & (dest_t < low + ROWS)
        first = jnp.min(jnp.where(inside, dest_t, 1e9), axis=0, keepdims=True)
        last = jnp.max(jnp.where(inside, dest_t, -1.0), axis=0, keepdims=True)
        pos_rows.append((first, last))
    for k in range(4):
        for r in range(2):
            pos_k = pos_rows[k][r]
            mask[:, (2 * k + r) * N:(2 * k + r + 1) * N] = jnp.where(
                (pos_k >= start) & (pos_k <= pos_q), 0.0, -1e30
            )
    for r in range(2):
        back[:, r * N:(r + 1) * N] = (iota((ROWS, N), 0) == pos_rows[3][r] - base).astype(BF)
    vals2[:, HD:] = jnp.ones((KEYS, HD), BF)

    def spread_q(g, carry):
        def one(i, inner):
            to = (me + i) & (N - 1)
            remote(
                send_q.at[g, pl.ds(pl.multiple_of(to * 16, 16), 16)],
                got_q.at[g, pl.ds(pl.multiple_of(me * 16, 16), 16)],
                q_send.at[g], q_recv.at[g], device_of(to),
            ).start()
            return inner

        return lax.fori_loop(1, N, one, carry, unroll=8)

    await_bytes(pre_k.at[:, 0, pl.ds(0, 3)], pre_recv.at[2])
    await_bytes(pre_v.at[:, pl.ds(0, 3), 0], pre_recv.at[3])
    spread_prefix(0, 81)
    spread_kv_part(0, 105, N)
    lax.fori_loop(0, HALF, spread_q, 0)
    spread_kv_part(1, 1, 41)
    spread_prefix(1, 41)
    spread_kv_part(1, 65, N)
    lax.fori_loop(HALF, LATE, spread_q, 0)

    def unpack_kv(h):
        def one(p, carry):
            stage_kv[0] = got_kv[h, pl.ds(pl.multiple_of(p * 2048, 2048), 2048), :].astype(F32)
            for x in range(8):
                for kr in range(8):
                    near[x // HALF, h * HALF + x % HALF, pl.ds(pl.multiple_of(kr * N + p * 32, 32), 32), :] = (
                        stage_kv[0, pl.ds(kr * 8 + x, 32, stride=64), :].astype(BF)
                    )
            return carry

        await_bytes(got_kv.at[h, pl.ds(0, (N - 1) * 64)], kv_recv.at[h])
        lax.fori_loop(0, 4, one, 0)
        await_bytes(pre_k.at[h, pl.ds(0, 3)], pre_recv.at[4 + 2 * h])
        await_bytes(pre_v.at[h, :, pl.ds(0, 3)], pre_recv.at[5 + 2 * h])

    def attend(g, carry):
        h = g >> 2
        columns = pl.ds(pl.multiple_of((g & 3) * HD, HD), HD)
        for y in range(4):
            prefix_keys = pre_k[h, y, :, :, :, columns].reshape(256, HD)
            rows = pl.ds(y * 256, 256)
            keys2[rows, :HD] = prefix_keys
            keys2[rows, HD:] = prefix_keys
            vals2[rows, :HD] = pre_v[h, y, :, :, :, columns].reshape(256, HD)
        keys2[PRE:, :HD] = near[0, g]
        keys2[PRE:, HD:] = near[0, g]
        vals2[PRE:, :HD] = near[1, g]
        await_bytes(got_q.at[g, pl.ds(0, (N - 1) * 16)], q_recv.at[g])
        stage_q[...] = got_q[g].astype(F32)
        for j in range(PER):
            for r in range(2):
                scaled = stage_q[pl.ds(r * PER + j, N, stride=16), :] * SCALE
                high = scaled.astype(BF)
                rows = pl.ds(j * ROWS + r * N, N)
                lhs[rows, :HD] = high
                lhs[rows, HD:] = (scaled - high.astype(F32)).astype(BF)

        def score_step(tile, into, peak, c, top):
            part = lax.dot_general(
                lhs[pl.ds(tile * TILE, TILE), :], keys2[c * WIDE:(c + 1) * WIDE, :],
                (((1,), (1,)), ((), ())), preferred_element_type=F32,
            )
            if c * WIDE >= PRE:
                allowed = mask[:, c * WIDE - PRE:(c + 1) * WIDE - PRE]
                part = part + jnp.concatenate([allowed] * (TILE // ROWS), axis=0)
            into[:, c * WIDE:(c + 1) * WIDE] = part
            for t in range(WIDE // HD):
                piece = part[:, t * HD:(t + 1) * HD]
                top = piece if top is None else jnp.maximum(top, piece)
            if c == KEYS // WIDE - 1:
                peak[...] = jnp.broadcast_to(jnp.max(top, axis=1, keepdims=True), (TILE, HD))
            return top

        def value_step(held, top, c, total):
            shifted = held[:, c * WIDE:(c + 1) * WIDE] - jnp.concatenate([top] * (WIDE // HD), axis=1)
            more = jnp.dot(
                jnp.exp2(shifted).astype(BF), vals2[c * WIDE:(c + 1) * WIDE, :],
                preferred_element_type=F32,
            )
            return more if total is None else total + more

        slots = ((scores_a, peak_a), (scores_b, peak_b))
        for tile in range(TILES + 1):
            into, peak = slots[tile % 2]
            held, held_peak = slots[(tile + 1) % 2]
            top = total = None
            before = held_peak[...] if tile > 0 else None
            for c in range(KEYS // WIDE):
                if tile < TILES:
                    top = score_step(tile, into, peak, c, top)
                if tile > 0:
                    total = value_step(held, before, c, total)
            if tile > 0:
                result = (total[:, :HD] / total[:, HD:]).astype(BF)
                for t in range(TILE // ROWS):
                    j = (tile - 1) * (TILE // ROWS) + t
                    heads_out[:, j * HD:(j + 1) * HD] = result[t * ROWS:(t + 1) * ROWS]
        out_ref[:, pl.ds(pl.multiple_of(g * 1024, 1024), 1024)] = jnp.dot(
            back[...], heads_out[...], preferred_element_type=F32
        ).astype(BF)
        return carry

    unpack_kv(0)
    lax.fori_loop(LATE, GROUPS, spread_q, 0)

    def attend_next(g, carry):
        @pl.when(g == HALF)
        def second_half():
            unpack_kv(1)

        return attend(g, carry)

    lax.fori_loop(0, GROUPS, attend_next, 0)

    def sent_q(g, carry):
        await_bytes(send_q.at[g, pl.ds(0, (N - 1) * 16)], q_send.at[g])
        return carry

    lax.fori_loop(0, GROUPS, sent_q, 0)
    for i, ref in enumerate((pre_k, pre_v)):
        await_bytes(ref.at[:, 0, 0, 0], pre_send.at[i])
    await_bytes(pre_k.at[:, 0, pl.ds(0, 3)], pre_send.at[2])
    await_bytes(pre_v.at[:, pl.ds(0, 3), 0], pre_send.at[3])
    for h in range(2):
        await_bytes(got_kv.at[h, pl.ds(0, (N - 1) * 64)], kv_send.at[h])
        await_bytes(pre_k.at[h, pl.ds(0, 3)], pre_send.at[4 + 2 * h])
        await_bytes(pre_v.at[h, :, pl.ds(0, 3)], pre_send.at[5 + 2 * h])


def per_device(resp_q, resp_k, resp_v, prefix_k, prefix_v, destination, resp_len):
    dest = destination.reshape(N, ROWS)
    vmem = pl.BlockSpec(memory_space=pltpu.VMEM)
    return pl.pallas_call(
        kernel,
        out_shape=jax.ShapeDtypeStruct((ROWS, GROUPS * PER * HD), BF),
        in_specs=[vmem] * 7 + [pl.BlockSpec(memory_space=pltpu.SMEM)],
        out_specs=vmem,
        scratch_shapes=[
            pltpu.VMEM((GROUPS, N * 16, HD), BF),
            pltpu.VMEM((2, 131 * 16, HD), BF),
            pltpu.VMEM((GROUPS, N * 16, HD), BF),
            pltpu.VMEM((2, N * 64, HD), BF),
            pltpu.VMEM((2, 4, 4, 2, 32, HALF * HD), BF),
            pltpu.VMEM((2, 4, 4, 2, 32, HALF * HD), BF),
            pltpu.VMEM((N * 16, HD), F32),
            pltpu.VMEM((2, N * 16, HD), F32),
            pltpu.VMEM((2, GROUPS, NEAR, HD), BF),
            pltpu.VMEM((PER * ROWS, 2 * HD), BF),
            pltpu.VMEM((KEYS, 2 * HD), BF),
            pltpu.VMEM((KEYS, 2 * HD), BF),
            pltpu.VMEM((ROWS, NEAR), F32),
            pltpu.VMEM((ROWS, ROWS), BF),
            pltpu.VMEM((TILE, KEYS), F32),
            pltpu.VMEM((TILE, KEYS), F32),
            pltpu.VMEM((TILE, HD), F32),
            pltpu.VMEM((TILE, HD), F32),
            pltpu.VMEM((ROWS, PER * HD), BF),
            pltpu.SemaphoreType.DMA((GROUPS,)),
            pltpu.SemaphoreType.DMA((GROUPS,)),
            pltpu.SemaphoreType.DMA((2,)),
            pltpu.SemaphoreType.DMA((2,)),
            pltpu.SemaphoreType.DMA((8,)),
            pltpu.SemaphoreType.DMA((8,)),
        ],
        compiler_params=pltpu.CompilerParams(
            collective_id=0, has_side_effects=True, vmem_limit_bytes=60 * 1024 * 1024
        ),
    )(resp_q, resp_k, resp_v, prefix_k, prefix_v, dest, dest.T, resp_len)


def solution(mesh):
    both = P(("prompt", "seq"), None)
    return jax.shard_map(
        per_device,
        mesh=mesh,
        in_specs=(both, both, both, both, both, P(), P("prompt", None)),
        out_specs=both,
        check_vma=False,
    )
```

time: 245 us -> 169 us (0.69)
  the two profiles are of different devices: /device:TPU:24 before, /device:TPU:8 now
where the time goes in v2:
time: 169 us
  Pallas kernels  162 us (96%)
  local copies, waits for them, and re-layouts  6.34 us (4%)
    pallas_call x1, Pallas kernels, per_device(): pl.pallas_call(kernel, out_shape=jax.ShapeDtypeStruct((ROWS, GROUPS * PER...  162 us
    unnamed x3, local copies, waits for them, and re-layouts  4.65 us

profile of v2, /device:TPU:8, one launch (start us, length us, event | category | flops | bytes accessed | tf_op | source)
XLA Modules:
  0.0 168.7 jit_solution(9270352446144005790)
XLA Ops:
  0.0 0.9 reshape.3.dest_ref
  0.9 0.0 copy-start
  1.0 0.8 copy.9
  1.7 0.0 copy-done
  1.7 162.3 %shard_map.73 = bf16[256,8192]{1,0:T(8,128)(2,1)} custom-call(bf16[256,8192]{1,0:T(8,128)(2,1)} %q_ref.1, bf16[256,1024]{1,0:T(8,128)(2,1)} %k_ref.1, bf16[256,1024]{1,0:T(8,128)(2,1)} %v_ref.1, bf16[32,1024]{1,0:T(8,128)(2,1)} %pk_ref.1, bf16[32,1024]{1,0:T(8,128)(2,1)} %pv_ref.1, s32[128,256]{1,0:T(8,128)} %copy-done, s32[256,128]{1,0:T(8,128)} %bitcast.1, ...), custom_call_target="tpu_custom_call" | custom-call | tf_op jit(solution)/shard_map/pallas_call | solution.py:325
  164.1 4.6 %copy.11 = bf16[256,8192]{1,0:T(8,128)(2,1)} copy(bf16[256,8192]{1,0:T(8,128)(2,1)} %shard_map.73) | data formatting | bytes 8388608
Async XLA Ops:
  0.9 0.8 copy-start

commit v3 on v2

--- a/solution.py
+++ b/solution.py
@@ -47,11 +47,14 @@
 
 
 def kernel(
-    q_ref, k_ref, v_ref, pk_ref, pv_ref, dest_ref, dest_t_ref, len_ref, out_ref,
+    q_hbm, k_ref, v_ref, pk_ref, pv_ref, dest_ref, dest_t_ref, len_ref, out_hbm,
+    q_ref, out_ref,
     send_q, send_kv, got_q, got_kv, pre_k, pre_v, stage_q, stage_kv, near,
     lhs, keys2, vals2, mask, back, scores_a, scores_b, peak_a, peak_b, heads_out,
-    q_send, q_recv, kv_send, kv_recv, pre_send, pre_recv,
+    q_send, q_recv, kv_send, kv_recv, pre_send, pre_recv, in_sem, out_sem,
 ):
+    load_q = pltpu.make_async_copy(q_hbm, q_ref, in_sem)
+    load_q.start()
     mp = lax.axis_index("prompt")
     ms = lax.axis_index("seq")
     me = mp * NS + ms
@@ -152,6 +155,7 @@
         got_q[g, own, :] = send_q[g, own, :]
         return carry
 
+    load_q.wait()
     lax.fori_loop(0, GROUPS, pack, 0)
 
     dest = dest_ref[...].astype(F32)
@@ -225,6 +229,10 @@
         await_bytes(pre_k.at[h, pl.ds(0, 3)], pre_recv.at[4 + 2 * h])
         await_bytes(pre_v.at[h, :, pl.ds(0, 3)], pre_recv.at[5 + 2 * h])
 
+    def store_out(g):
+        columns = pl.ds(pl.multiple_of(g * 1024, 1024), 1024)
+        return pltpu.make_async_copy(out_ref.at[:, columns], out_hbm.at[:, columns], out_sem.at[g])
+
     def attend(g, carry):
         h = g >> 2
         columns = pl.ds(pl.multiple_of((g & 3) * HD, HD), HD)
@@ -290,6 +298,7 @@
         out_ref[:, pl.ds(pl.multiple_of(g * 1024, 1024), 1024)] = jnp.dot(
             back[...], heads_out[...], preferred_element_type=F32
         ).astype(BF)
+        store_out(g).start()
         return carry
 
     unpack_kv(0)
@@ -305,6 +314,7 @@
     lax.fori_loop(0, GROUPS, attend_next, 0)
 
     def sent_q(g, carry):
+        store_out(g).wait()
         await_bytes(send_q.at[g, pl.ds(0, (N - 1) * 16)], q_send.at[g])
         return carry
 
@@ -322,12 +332,15 @@
 def per_device(resp_q, resp_k, resp_v, prefix_k, prefix_v, destination, resp_len):
     dest = destination.reshape(N, ROWS)
     vmem = pl.BlockSpec(memory_space=pltpu.VMEM)
+    anywhere = pl.BlockSpec(memory_space=pl.ANY)
     return pl.pallas_call(
         kernel,
         out_shape=jax.ShapeDtypeStruct((ROWS, GROUPS * PER * HD), BF),
-        in_specs=[vmem] * 7 + [pl.BlockSpec(memory_space=pltpu.SMEM)],
-        out_specs=vmem,
+        in_specs=[anywhere] + [vmem] * 6 + [pl.BlockSpec(memory_space=pltpu.SMEM)],
+        out_specs=anywhere,
         scratch_shapes=[
+            pltpu.VMEM((ROWS, GROUPS * PER * HD), BF),
+            pltpu.VMEM((ROWS, GROUPS * PER * HD), BF),
             pltpu.VMEM((GROUPS, N * 16, HD), BF),
             pltpu.VMEM((2, 131 * 16, HD), BF),
             pltpu.VMEM((GROUPS, N * 16, HD), BF),
@@ -353,6 +366,8 @@
             pltpu.SemaphoreType.DMA((2,)),
             pltpu.SemaphoreType.DMA((8,)),
             pltpu.SemaphoreType.DMA((8,)),
+            pltpu.SemaphoreType.DMA,
+            pltpu.SemaphoreType.DMA((GROUPS,)),
         ],
         compiler_params=pltpu.CompilerParams(
             collective_id=0, has_side_effects=True, vmem_limit_bytes=60 * 1024 * 1024

time: 169 us -> 167 us (0.988)
  Pallas kernels: 162 us -> 160 us
    pallas_call x1, Pallas kernels: 162 us -> 160 us  [per_device(): pl.pallas_call(kernel, out_shape=jax.ShapeDtypeStruct((ROWS, GROUPS * PER...]
where the time goes in v3:
time: 167 us; the launch traced here: 166 us
  Pallas kernels  160 us (96%)
  local copies, waits for them, and re-layouts  6.34 us (4%)
    pallas_call x1, Pallas kernels, per_device(): pl.pallas_call(kernel, out_shape=jax.ShapeDtypeStruct((ROWS, GROUPS * PER...  160 us
    unnamed x3, local copies, waits for them, and re-layouts  4.65 us

profile of v3, /device:TPU:8, one launch (start us, length us, event | category | flops | bytes accessed | tf_op | source)
XLA Modules:
  0.0 166.4 jit_solution(11055298206376987535)
XLA Ops:
  0.0 0.9 reshape.3.dest_ref
  0.9 0.0 copy-start
  1.0 0.8 copy.9
  1.7 0.0 copy-done
  1.7 160.0 %shard_map.73 = bf16[256,8192]{1,0:T(8,128)(2,1)} custom-call(bf16[256,8192]{1,0:T(8,128)(2,1)} %q_hbm.1, bf16[256,1024]{1,0:T(8,128)(2,1)} %k_ref.1, bf16[256,1024]{1,0:T(8,128)(2,1)} %v_ref.1, bf16[32,1024]{1,0:T(8,128)(2,1)} %pk_ref.1, bf16[32,1024]{1,0:T(8,128)(2,1)} %pv_ref.1, s32[128,256]{1,0:T(8,128)} %copy-done, s32[256,128]{1,0:T(8,128)} %bitcast.1, ...), custom_call_target="tpu_custom_call" | custom-call | tf_op jit(solution)/shard_map/pallas_call | solution.py:336
  161.7 4.6 %copy.11 = bf16[256,8192]{1,0:T(8,128)(2,1)} copy(bf16[256,8192]{1,0:T(8,128)(2,1)} %shard_map.73) | data formatting | bytes 8388608
Async XLA Ops:
  0.9 0.8 copy-start

commit v4 on v3

--- a/solution.py
+++ b/solution.py
@@ -23,7 +23,7 @@
 TILES = PER * ROWS // TILE
 SCALE = math.log2(math.e) / math.sqrt(HD)
 HALF = 4
-LATE = 8
+FIRST = 2
 BF = jnp.bfloat16
 F32 = jnp.float32
 
@@ -208,11 +208,11 @@
     await_bytes(pre_v.at[:, pl.ds(0, 3), 0], pre_recv.at[3])
     spread_prefix(0, 81)
     spread_kv_part(0, 105, N)
-    lax.fori_loop(0, HALF, spread_q, 0)
+    lax.fori_loop(0, FIRST, spread_q, 0)
     spread_kv_part(1, 1, 41)
     spread_prefix(1, 41)
     spread_kv_part(1, 65, N)
-    lax.fori_loop(HALF, LATE, spread_q, 0)
+    lax.fori_loop(FIRST, GROUPS, spread_q, 0)
 
     def unpack_kv(h):
         def one(p, carry):
@@ -302,7 +302,6 @@
         return carry
 
     unpack_kv(0)
-    lax.fori_loop(LATE, GROUPS, spread_q, 0)
 
     def attend_next(g, carry):
         @pl.when(g == HALF)

time: 167 us -> 172 us (1.030)
  Pallas kernels: 160 us -> 164 us
    pallas_call x1, Pallas kernels: 160 us -> 164 us  [per_device(): pl.pallas_call(kernel, out_shape=jax.ShapeDtypeStruct((ROWS, GROUPS * PER...]
where the time goes in v4:
time: 172 us; the launch traced here: 171 us
  Pallas kernels  164 us (95%)
  local copies, waits for them, and re-layouts  6.34 us (4%)
    pallas_call x1, Pallas kernels, per_device(): pl.pallas_call(kernel, out_shape=jax.ShapeDtypeStruct((ROWS, GROUPS * PER...  164 us
    unnamed x3, local copies, waits for them, and re-layouts  4.65 us

profile of v4, /device:TPU:8, one launch (start us, length us, event | category | flops | bytes accessed | tf_op | source)
XLA Modules:
  0.0 170.7 jit_solution(5083178715386565115)
XLA Ops:
  0.0 0.9 reshape.3.dest_ref
  0.9 0.0 copy-start
  1.0 0.8 copy.9
  1.7 0.0 copy-done
  1.7 164.4 %shard_map.73 = bf16[256,8192]{1,0:T(8,128)(2,1)} custom-call(bf16[256,8192]{1,0:T(8,128)(2,1)} %q_hbm.1, bf16[256,1024]{1,0:T(8,128)(2,1)} %k_ref.1, bf16[256,1024]{1,0:T(8,128)(2,1)} %v_ref.1, bf16[32,1024]{1,0:T(8,128)(2,1)} %pk_ref.1, bf16[32,1024]{1,0:T(8,128)(2,1)} %pv_ref.1, s32[128,256]{1,0:T(8,128)} %copy-done, s32[256,128]{1,0:T(8,128)} %bitcast.1, ...), custom_call_target="tpu_custom_call" | custom-call | tf_op jit(solution)/shard_map/pallas_call | solution.py:335
  166.1 4.6 %copy.11 = bf16[256,8192]{1,0:T(8,128)(2,1)} copy(bf16[256,8192]{1,0:T(8,128)(2,1)} %shard_map.73) | data formatting | bytes 8388608
Async XLA Ops:
  0.9 0.8 copy-start
